TPU v7x, 32 devices: a whole 2x2x4 slice. The times are simulated.
32 devices in a mesh: dp: 8 (over z, x), fsdp: 4 (over y, core).
Axes of the slice: x: 2, y: 2, z: 4, core: 2. Of those that a mesh axis runs over, the one named last changes fastest.
Arguments:
- tokens: bfloat16 [65536, 768], P(('dp', 'fsdp')), may hold values from -6 to 6
- norm_gain: bfloat16 [768], P(('dp', 'fsdp')), may hold values from 0.099609375 to 1.8984375
- in_weight: bfloat16 [768, 3352], P(('dp', 'fsdp')), may hold values from -0.21875 to 0.21875
- conv_weight: bfloat16 [4, 1792], P(None, ('dp', 'fsdp')), may hold values from -3 to 3
- conv_bias: bfloat16 [1792], P(('dp', 'fsdp')), may hold values from -3 to 3
- decay_log: float32 [24], replicated, may hold values from 0 to 2.77
- step_bias: float32 [24], replicated, may hold values from -6.9 to -2.3
- skip_gain: float32 [24], replicated, may hold values from 0.5 to 1.5
- gate_gain: bfloat16 [1536], P(('dp', 'fsdp')), may hold values from 0.099609375 to 1.8984375
- out_weight: bfloat16 [1536, 768], P(('dp', 'fsdp')), may hold values from -0.15625 to 0.15625
- span_start: int32 [256], P(('dp', 'fsdp')), may hold values from 0 to 1, as said below
- span_valid: int32 [256], P(('dp', 'fsdp')), may hold values from 1 to 256, as said below
- cotangent: bfloat16 [65536, 768], P(('dp', 'fsdp')), may hold values from -6 to 6
Outputs:
- output: bfloat16 [65536, 768], P(('dp', 'fsdp'))
- tokens_grad: bfloat16 [65536, 768], P(('dp', 'fsdp'))
- norm_gain_grad: float32 [768], P(('dp', 'fsdp'))
- in_weight_grad: float32 [768, 3352], P(('dp', 'fsdp'))
- conv_weight_grad: float32 [4, 1792], P(None, ('dp', 'fsdp'))
- conv_bias_grad: float32 [1792], P(('dp', 'fsdp'))
- decay_log_grad: float32 [24], replicated
- step_bias_grad: float32 [24], replicated
- skip_gain_grad: float32 [24], replicated
- gate_gain_grad: float32 [1536], P(('dp', 'fsdp'))
- out_weight_grad: float32 [1536, 768], P(('dp', 'fsdp'))
Inputs may be any that keep to these rules, and one draw needn't show every extreme that they name: `span_start`: each device's first span begins a sequence, so a sequence's spans lie on one device; the first device holds a single sequence over all its 8 spans. `span_valid`: every span but a sequence's last holds 256 live tokens; a sequence's last span holds 1 to 256.
All inputs are finite; a program needn't handle non-finite values.
Results may differ from a plain program's by a relative error of at most 0.008.
Values may be sent and summed in bfloat16 or wider, within the bound.
A program may use at most 320 MiB of HBM per device.

v0:
```python
import jax
import jax.numpy as jnp
from jax import lax
from jax.sharding import PartitionSpec as P

precise = lax.Precision.HIGHEST
epsilon = 1e-05


def rms_scale(values):
    return values * lax.rsqrt(jnp.mean(values * values, axis=-1, keepdims=True) + epsilon)


def causal_conv(signal, conv_taps, conv_shift, span_start):
    spans = signal.shape[0]
    length = signal.shape[1]
    width = signal.shape[2]
    tap_count = conv_taps.shape[0]
    flat = signal.reshape(spans * length, width)
    offsets = jnp.arange(length, dtype=jnp.int32)
    total = conv_shift[None, None, :] + conv_taps[tap_count - 1][None, None, :] * signal
    for shift_by in range(1, tap_count):
        moved = jnp.concatenate(
            [jnp.zeros((shift_by, width), jnp.float32), flat[:-shift_by]], axis=0
        )
        moved = moved.reshape(spans, length, width)
        allowed = jnp.logical_or(offsets[None, :] >= shift_by, span_start[:, None] == 0).astype(
            jnp.float32
        )
        total = (
            total + conv_taps[tap_count - 1 - shift_by][None, None, :] * moved * allowed[:, :, None]
        )
    return total


def span_scan(values, step_sizes, rates, into_state, read_state, span_start):
    length = values.shape[1]
    heads = values.shape[2]
    head_dim = values.shape[3]
    running = jnp.cumsum(jnp.swapaxes(step_sizes * rates[None, None, :], 1, 2), axis=2)
    weighted = values * step_sizes[:, :, :, None]
    offsets = jnp.arange(length, dtype=jnp.int32)
    lower = (offsets[:, None] >= offsets[None, :])[None, None, :, :]
    spread = running[:, :, :, None] - running[:, :, None, :]
    within = jnp.where(lower, jnp.exp(jnp.where(lower, spread, 0.0)), 0.0)
    intersections = jnp.einsum("cin,cjn->cij", read_state, into_state, precision=precise)
    mixing = within * intersections[:, None, :, :]
    inside = jnp.einsum("chij,cjhp->cihp", mixing, weighted, precision=precise)
    leaving = jnp.exp(running[:, :, -1:] - running)
    deposits = jnp.einsum("chj,cjn,cjhp->chpn", leaving, into_state, weighted, precision=precise)
    carried = jnp.exp(running[:, :, -1])

    def advance(state, pieces):
        begin, deposit, factor = pieces
        entering = jnp.where(begin == 1, jnp.zeros_like(state), state)
        return (factor[:, None, None] * entering + deposit, entering)

    initial = jnp.zeros((heads, head_dim, into_state.shape[-1]), jnp.float32)
    final_state, entering = lax.scan(advance, initial, (span_start, deposits, carried))
    outside = jnp.einsum(
        "cin,chpn,chi->cihp", read_state, entering, jnp.exp(running), precision=precise
    )
    return inside + outside


def mixer(projected, conv_taps, conv_shift, decay_log, step_bias, skip_gain, gate_gain, span_start):
    spans = projected.shape[0]
    length = projected.shape[1]
    inner = gate_gain.shape[0]
    channels = conv_shift.shape[0]
    state_width = (channels - inner) // 2
    heads = decay_log.shape[0]
    head_dim = inner // heads
    gate_part = projected[:, :, :inner]
    conv_part = projected[:, :, inner : inner + channels]
    step_part = projected[:, :, inner + channels :]
    convolved = jax.nn.silu(causal_conv(conv_part, conv_taps, conv_shift, span_start))
    values = convolved[:, :, :inner].reshape(spans, length, heads, head_dim)
    into_state = convolved[:, :, inner : inner + state_width]
    read_state = convolved[:, :, inner + state_width :]
    step_sizes = jax.nn.softplus(step_part + step_bias[None, None, :])
    rates = -jnp.exp(decay_log)
    scanned = span_scan(values, step_sizes, rates, into_state, read_state, span_start)
    scanned = scanned + skip_gain[None, None, :, None] * values
    mixed = scanned.reshape(spans, length, inner) * jax.nn.silu(gate_part)
    return rms_scale(mixed) * gate_gain


def collect(gain_norm, weight_in, conv_taps, conv_shift, gain_gate, weight_out):
    whole = (
        lax.all_gather(gain_norm, ("dp", "fsdp"), axis=0, tiled=True),
        lax.all_gather(weight_in, ("dp", "fsdp"), axis=0, tiled=True),
        lax.all_gather(conv_taps, ("dp", "fsdp"), axis=1, tiled=True),
        lax.all_gather(conv_shift, ("dp", "fsdp"), axis=0, tiled=True),
        lax.all_gather(gain_gate, ("dp", "fsdp"), axis=0, tiled=True),
        lax.all_gather(weight_out, ("dp", "fsdp"), axis=0, tiled=True),
    )
    return whole


def spread_back(grad_norm, grad_in, grad_taps, grad_shift, grad_gate, grad_out):
    shares = (
        lax.psum_scatter(grad_norm, ("dp", "fsdp"), scatter_dimension=0, tiled=True),
        lax.psum_scatter(grad_in, ("dp", "fsdp"), scatter_dimension=0, tiled=True),
        lax.psum_scatter(grad_taps, ("dp", "fsdp"), scatter_dimension=1, tiled=True),
        lax.psum_scatter(grad_shift, ("dp", "fsdp"), scatter_dimension=0, tiled=True),
        lax.psum_scatter(grad_gate, ("dp", "fsdp"), scatter_dimension=0, tiled=True),
        lax.psum_scatter(grad_out, ("dp", "fsdp"), scatter_dimension=0, tiled=True),
    )
    return shares


def per_device(
    tokens,
    norm_gain,
    in_weight,
    conv_weight,
    conv_bias,
    decay_log,
    step_bias,
    skip_gain,
    gate_gain,
    out_weight,
    span_start,
    span_valid,
    cotangent,
):
    spans = span_start.shape[0]
    length = tokens.shape[0] // spans
    offsets = jnp.arange(length, dtype=jnp.int32)
    live = (offsets[None, :] < span_valid[:, None]).astype(jnp.float32).reshape(-1, 1)
    gathered = collect(norm_gain, in_weight, conv_weight, conv_bias, gate_gain, out_weight)
    full_norm = gathered[0]
    full_in = gathered[1]
    full_taps = gathered[2]
    full_shift = gathered[3]
    full_gate = gathered[4]
    full_out = gathered[5]
    rows = tokens.astype(jnp.float32)

    def pre_norm(values, gain):
        return rms_scale(values) * gain

    normed, pre_back = jax.vjp(pre_norm, rows, full_norm.astype(jnp.float32))
    normed_low = normed.astype(jnp.bfloat16)
    projected = jnp.dot(normed_low, full_in, preferred_element_type=jnp.float32)

    def middle(values, conv_taps, conv_shift, decay, bias_step, skip, gain):
        shaped = values.reshape(spans, length, values.shape[1])
        mixed = mixer(shaped, conv_taps, conv_shift, decay, bias_step, skip, gain, span_start)
        return mixed.reshape(values.shape[0], -1)

    gated, middle_back = jax.vjp(
        middle,
        projected,
        full_taps.astype(jnp.float32),
        full_shift.astype(jnp.float32),
        decay_log,
        step_bias,
        skip_gain,
        full_gate.astype(jnp.float32),
    )
    gated_low = gated.astype(jnp.bfloat16)
    branch = jnp.dot(gated_low, full_out, preferred_element_type=jnp.float32)
    output = (rows + branch * live).astype(jnp.bfloat16)
    again = collect(norm_gain, in_weight, conv_weight, conv_bias, gate_gain, out_weight)
    back_in = again[1]
    back_out = again[5]
    flowing = cotangent.astype(jnp.float32)
    branch_grad = (flowing * live).astype(jnp.bfloat16)
    out_grad = lax.dot_general(
        gated_low, branch_grad, (((0,), (0,)), ((), ())), preferred_element_type=jnp.float32
    )
    gated_grad = lax.dot_general(
        branch_grad, back_out, (((1,), (1,)), ((), ())), preferred_element_type=jnp.float32
    )
    proj_grad, taps_grad, shift_grad, decay_grad, step_grad, skip_grad, gain_grad = middle_back(
        gated_grad
    )
    proj_low = proj_grad.astype(jnp.bfloat16)
    in_grad = lax.dot_general(
        normed_low, proj_low, (((0,), (0,)), ((), ())), preferred_element_type=jnp.float32
    )
    normed_grad = lax.dot_general(
        proj_low, back_in, (((1,), (1,)), ((), ())), preferred_element_type=jnp.float32
    )
    rows_grad, norm_grad = pre_back(normed_grad)
    token_grad = (flowing + rows_grad).astype(jnp.bfloat16)
    shares = spread_back(norm_grad, in_grad, taps_grad, shift_grad, gain_grad, out_grad)
    head_sums = lax.psum((decay_grad, step_grad, skip_grad), ("dp", "fsdp"))
    return (
        output,
        token_grad,
        shares[0],
        shares[1],
        shares[2],
        shares[3],
        head_sums[0],
        head_sums[1],
        head_sums[2],
        shares[4],
        shares[5],
    )


def solution(mesh):
    in_specs = (
        P(("dp", "fsdp"), None),
        P(("dp", "fsdp")),
        P(("dp", "fsdp"), None),
        P(None, ("dp", "fsdp")),
        P(("dp", "fsdp")),
        P(),
        P(),
        P(),
        P(("dp", "fsdp")),
        P(("dp", "fsdp"), None),
        P(("dp", "fsdp")),
        P(("dp", "fsdp")),
        P(("dp", "fsdp"), None),
    )
    out_specs = (
        P(("dp", "fsdp"), None),
        P(("dp", "fsdp"), None),
        P(("dp", "fsdp")),
        P(("dp", "fsdp"), None),
        P(None, ("dp", "fsdp")),
        P(("dp", "fsdp")),
        P(),
        P(),
        P(),
        P(("dp", "fsdp")),
        P(("dp", "fsdp"), None),
    )
    return jax.shard_map(
        per_device, mesh=mesh, in_specs=in_specs, out_specs=out_specs, check_vma=False
    )
```

profile of v0, /device:TPU:0, one launch (start us, length us, event | category | flops | bytes accessed | tf_op | source)
XLA Modules:
  0.0 1117.7 jit_solution(10307887816391400687)
XLA Ops:
  11.3 42.3 %all-reduce.27 = (bf16[768]{0:T(1024)(128)(2,1)S(1)}, bf16[1792]{0:T(1024)(128)(2,1)S(1)}, bf16[1536]{0:T(1024)(128)(2,1)S(1)}) all-reduce(bf16[768]{0:T(1024)(128)(2,1)S(1)} %dynamic-update-slice.1, bf16[1792]{0:T(1024)(128)(2,1)S(1)} %dynamic-update-slice, ...), channel_id=1, replica_groups=mesh['dp'=8,'fsdp'=4] {'dp','fsdp'}, use_global_device_ids=true, to_apply=%add.19 | all-reduce | flops 4096 | bytes 16384
  53.6 40.8 %all-gather = bf16[32,56,4]{1,2,0:T(4,128)(2,1)S(1)} all-gather(bf16[1,56,4]{1,2,0:T(4,128)(2,1)} %bitcast.264), channel_id=1, replica_groups=mesh['dp'=8,'fsdp'=4] {'dp','fsdp'}, dimensions={0}, use_global_device_ids=true | all-gather | bytes 14784 | tf_op jit(solution)/shard_map/all_gather | solution.py:93
  110.9 27.5 %all-gather.4.cloned.1.call-done = bf16[768,3352]{1,0:T(8,128)(2,1)} async-done(((bf16[24,3352]{1,0:T(8,128)(2,1)}), bf16[768,3352]{1,0:T(8,128)(2,1)}) %all-gather.4.cloned.1.call-update) | async-done | bytes 5148688 | tf_op jit(solution)/shard_map/all_gather | solution.py:92
  138.4 19.8 %fusion.91 = f32[2048,3352]{1,0:T(8,128)} fusion(bf16[768,3352]{1,0:T(8,128)(2,1)} %all-gather.4.cloned.1.call-done, bf16[2048,768]{1,0:T(8,128)(2,1)} %param.17, f32[768]{0:T(1024)S(1)} %convert_element_type.76, f32[2048]{0:T(1024)S(1)} %fusion.109), kind=kOutput, calls=%fused_computation.134 | convolution fusion | flops 10550771712 | bytes 35765248 | tf_op jit(solution)/shard_map/jvp()/reshape | solution.py:149
  211.0 30.3 %fusion.24 = (f32[8,256,1792]{2,1,0:T(8,128)}, f32[8,256,1792]{2,1,0:T(8,128)}) fusion(f32[8,256]{1,0:T(8,128)S(1)} %get-tuple-element.358, f32[8,256,1792]{2,1,0:T(8,128)} %bitcast.241, f32[1792]{0:T(1024)S(1)} %get-tuple-element.288, f32[8,256]{1,0:T(8,128)S(1)} %get-tuple-element.357, f32[8,256,1792]{2,1,0:T(8,128)} %bitcast.243, ...), kind=kLoop, calls=%fused_computation.46 | loop fusion | flops 55050240 | bytes 88140800 | tf_op jit(solution)/shard_map/jvp(jit(silu))/mul | solution.py:77
  256.4 12.6 %copy.152 = f32[8,256,1536]{1,2,0:T(8,128)} copy(f32[8,256,1536]{2,1,0:T(8,128)} %slice.81) | data formatting | bytes 25165824 | tf_op jit(solution)/shard_map/jvp()/slice | solution.py:78
  281.5 16.5 %fusion.38 = f32[8,24,64,128]{3,2,1,0:T(8,128)} fusion(f32[8,256,24,64]{1,3,2,0:T(8,128)} %bitcast.217, f32[8,256,24]{1,2,0:T(8,128)S(1)} %get-tuple-element.355, f32[8,256,24]{1,2,0:T(8,128)S(1)} %copy.154, f32[8,256,1792]{2,1,0:T(8,128)} %get-tuple-element.340), kind=kOutput, calls=%fused_computation.81 | convolution fusion | flops 4838129664 | bytes 20316160 | tf_op jit(solution)/shard_map/jvp(chj,cjn,cjhp->chpn)/dot_general | solution.py:50
  301.5 39.6 %while.36 = (s32[]{:T(128)}, f32[24,64,128]{2,1,0:T(8,128)S(1)}, f32[8,24,64,128]{3,2,1,0:T(8,128)}, pred[8]{0:T(512)(128)(4,1)S(1)}, f32[8,24,1,1]{1,3,2,0:T(1,...) while((s32[]{:T(128)}, f32[24,64,128]{2,1,0:T(8,128)S(1)}, ...), condition=%wide.region_4.5_spmd.clone, body=%wide.region_3.4_spmd.clone.sunk | while | flops 1179652 | bytes 3934636 | solution.py:59
  341.1 13.4 %fusion.84 = f32[8,24,64,256]{3,2,1,0:T(8,128)S(1)} fusion(f32[8,24,64,128]{3,2,1,0:T(8,128)} %get-tuple-element.503, f32[8,256,1792]{2,1,0:T(8,128)} %get-tuple-element.340), kind=kOutput, calls=%fused_computation.128 | convolution fusion | flops 4831838208 | bytes 19922944 | tf_op jit(solution)/shard_map/jvp(cin,chpn,chi->cihp)/dot_general | solution.py:60
  354.6 62.3 %fusion.32 = f32[8,256,24,64]{1,3,2,0:T(8,128)} fusion(f32[8,24,64,256]{3,2,1,0:T(8,128)S(1)} %fusion.84, f32[8,256,24,64]{1,3,2,0:T(8,128)} %bitcast.218, f32[8,256,256]{2,1,0:T(8,128)S(1)} %copy-done.16, f32[8,24,256]{2,1,0:T(8,128)S(1)} %copy_bitcast_fusion, pred[256,256]{1,0:T(8,128)(4,1)S(1)} %iota_compare_fusion, f32[24]{0:T(128)S(1)} %copy-done.61, ...), kind=kOutput, calls=%fused_computation.60 | convolution fusion | flops 9726590976 | bytes 52887648 | tf_op jit(solution)/shard_map/jvp(chij,cjhp->cihp)/dot_general | solution.py:48
  416.9 12.6 %copy.160 = f32[8,256,1536]{2,1,0:T(8,128)} copy(f32[8,256,1536]{1,2,0:T(8,128)} %bitcast.253) | data formatting | bytes 25165824 | tf_op jit(solution)/shard_map/jvp()/reshape | solution.py:85
  439.4 14.7 %multiply_reduce_fusion.7 = (f32[1536]{0:T(1024)}, f32[8,256]{1,0:T(8,128)S(1)}) fusion(f32[8,256,1536]{2,1,0:T(8,128)S(1)} %get-tuple-element.339, f32[8,256]{1,0:T(8,128)S(1)} %fusion.110, f32[2048,1536]{1,0:T(8,128)} %fusion.76, f32[8,256,1536]{2,1,0:T(8,128)} %bitcast.240, f32[1536]{0:T(1024)S(1)} %copy-done.40), kind=kLoop, calls=%fused_computation.63 | loop fusion | flops 18870784 | bytes 37777408 | tf_op jit(solution)/shard_map/transpose(jvp())/reduce_sum | solution.py:86
  454.2 33.2 %multiply_reduce_fusion.8 = (f32[1536]{0:T(1024)}, f32[8,256,1536]{2,1,0:T(8,128)}, f32[8,256,1536]{2,1,0:T(8,128)}, bf16[8,256,1536]{2,1,0:T(8,128)(2,1)}) fusion(f32[8,256,1792]{2,1,0:T(8,128)} %get-tuple-element.340, f32[8,256,3352]{2,1,0:T(8,128)} %bitcast.235, f32[8,256,1536]{2,1,0:T(8,128)} %copy-done.1, f32[8,256]{1,0:T(8,128)S(1)} %multiply_multiply_fusion.4, ...), kind=kLoop, calls=%fused_computation.64 | loop fusion | flops 69204480 | bytes 94400512 | tf_op jit(solution)/shard_map/transpose(jvp())/reduce_sum | solution.py:84
  487.4 12.7 %copy.161 = f32[8,256,1536]{1,2,0:T(8,128)} copy(f32[8,256,1536]{2,1,0:T(8,128)} %get-tuple-element.334) | data formatting | bytes 25165824 | tf_op jit(solution)/shard_map/transpose(jvp())/mul | solution.py:85
  500.1 16.2 %fusion.29 = f32[8,24,64,128]{3,2,1,0:T(8,128)} fusion(f32[8,256,24,64]{1,3,2,0:T(8,128)} %bitcast.223, f32[8,256,24]{1,2,0:T(8,128)S(1)} %get-tuple-element.354, f32[8,256,1792]{2,1,0:T(8,128)} %get-tuple-element.340), kind=kOutput, calls=%fused_computation.56 | convolution fusion | flops 4834983936 | bytes 20119552 | tf_op jit(solution)/shard_map/transpose(jvp(cin,chpn,chi->cihp))/dot_general | solution.py:60
  516.2 22.9 %fusion.71 = f32[8,256,128]{2,1,0:T(8,128)} fusion(f32[8,24,64,128]{3,2,1,0:T(8,128)} %get-tuple-element.503, f32[8,256,24,64]{1,3,2,0:T(8,128)S(1)} %bitcast.227, f32[8,256,24]{1,2,0:T(8,128)S(1)} %get-tuple-element.354), kind=kOutput, calls=%fused_computation.114 | convolution fusion | flops 4834983936 | bytes 20119552 | tf_op jit(solution)/shard_map/transpose(jvp(cin,chpn,chi->cihp))/dot_general | solution.py:60
  542.6 31.4 %while.37 = (s32[]{:T(128)}, f32[24,64,128]{2,1,0:T(8,128)S(1)}, f32[8,24,64,128]{3,2,1,0:T(8,128)}, f32[8,24]{1,0:T(8,128)S(1)}, pred[8]{0:T(512)(128)(4,1)S(1)...) while((s32[]{:T(128)}, f32[24,64,128]{2,1,0:T(8,128)S(1)}, ...), condition=%wide.region_9.10_spmd.clone, body=%wide.region_7.9_spmd.clone.sunk | while | flops 1376236 | bytes 4719323 | solution.py:59
  574.1 18.8 %multiply_reduce_fusion.5 = (f32[8,24,256]{2,1,0:T(8,128)S(1)}, f32[8,256,24,64]{1,3,2,0:T(8,128)}) fusion(f32[8,256,24,64]{1,3,2,0:T(8,128)} %bitcast.219, f32[8,256,24]{1,2,0:T(8,128)S(1)} %copy.154, f32[8,24,64,128]{3,2,1,0:T(8,128)} %get-tuple-element.219, f32[8,256,1792]{2,1,0:T(8,128)} %get-tuple-element.340), kind=kOutput, calls=%fused_computation.61 | convolution fusion | flops 4841226240 | bytes 32899072 | tf_op jit(solution)/shard_map/transpose(jvp(chj,cjn,cjhp->chpn))/dot_general | solution.py:50
  592.9 23.9 %fusion.68 = f32[8,256,128]{2,1,0:T(8,128)} fusion(f32[8,24,64,128]{3,2,1,0:T(8,128)S(1)} %copy-done.3, f32[8,256,24,64]{1,3,2,0:T(8,128)} %bitcast.220, f32[8,256,24]{1,2,0:T(8,128)S(1)} %get-tuple-element.355, f32[8,256,24]{1,2,0:T(8,128)S(1)} %copy.154), kind=kOutput, calls=%fused_computation.113 | convolution fusion | flops 4838129664 | bytes 20316160 | tf_op jit(solution)/shard_map/transpose(jvp(chj,cjn,cjhp->chpn))/dot_general | solution.py:50
  624.6 73.3 %fusion.11 = (f32[8,24,256]{2,1,0:T(8,128)S(1)}, f32[8,24,256]{2,1,0:T(8,128)S(1)}, f32[8,256,256]{2,1,0:T(8,128)S(1)}) fusion(f32[8,256,256]{2,1,0:T(8,128)} %fusion.96, f32[8,24,256]{2,1,0:T(8,128)S(1)} %copy_bitcast_fusion, pred[256,256]{1,0:T(8,128)(4,1)S(1)} %iota_compare_fusion, f32[8,24,64,256]{3,2,1,0:T(8,128)} %bitcast.224, ...), kind=kOutput, calls=%fused_computation.22 | convolution fusion | flops 9804611584 | bytes 30212096 | tf_op jit(solution)/shard_map/transpose(jvp(chij,cjhp->cihp))/dot_general | solution.py:48
  698.2 19.9 %reduce-window.16 = f32[8,24,2,128]{3,1,2,0:T(8,128)S(1)} reduce-window(f32[8,24,2,128]{3,1,2,0:T(8,128)S(1)} %copy_bitcast_fusion.1, f32[]{:T(128)} %constant.108.clone.1), window={size=1x1x1x128 pad=0_0x0_0x0_0x0_127}, to_apply=%region_14.15 | reduce-window | flops 6242304 | bytes 393220 | tf_op jit(solution)/shard_map/reduce-window.2
  718.9 49.5 %multiply_reduce_fusion.9 = (f32[8,256,24]{1,2,0:T(8,128)S(1)}, f32[8,256,24,64]{1,3,2,0:T(8,128)}) fusion(f32[8,256,24,64]{1,3,2,0:T(8,128)} %bitcast.222, f32[8,256,24,64]{1,3,2,0:T(8,128)} %get-tuple-element.360, f32[8,256,24]{1,2,0:T(8,128)S(1)} %get-tuple-element.355, f32[8,256,24]{1,2,0:T(8,128)S(1)} %copy.154, f32[8,256,24,64]{1,3,2,0:T(8,128)} %bitcast.225, ...), kind=kOutput, calls=%fused_computation.66 | convolution fusion | flops 9735979008 | bytes 65863776 | tf_op jit(solution)/shard_map/transpose(jvp(chij,cjhp->cihp))/dot_general | solution.py:48
  777.3 12.7 %copy.170 = f32[8,256,1536]{2,1,0:T(8,128)} copy(f32[8,256,1536]{1,2,0:T(8,128)} %bitcast.252) | data formatting | bytes 25165824 | tf_op jit(solution)/shard_map/transpose(jvp())/reshape | solution.py:78
  790.0 38.1 %fusion.113 = (f32[1792]{0:T(1024)S(1)}, f32[1792]{0:T(1024)}, f32[1792]{0:T(1024)}, f32[1792]{0:T(1024)}, f32[1792]{0:T(1024)S(1)}, /*index=5*/f32[8,256,1792]{2,1,0:T(8,128)}) fusion(f32[2045,1792]{1,0:T(8,128)} %bitcast.213, f32[8,256]{1,0:T(8,128)S(1)} %copy-done.29, f32[2046,1792]{1,0:T(8,128)} %bitcast.214, f32[8,256]{1,0:T(8,128)S(1)} %copy-done.27, ...), kind=kLoop, calls=%fused_computation.188 | loop fusion | flops 84401408 | bytes 102777856 | tf_op jit(solution)/shard_map/transpose(jvp())/reduce_sum | solution.py:21
  828.1 19.3 %multiply_multiply_fusion.2 = (f32[8,256,1792]{2,1,0:T(8,128)}, f32[8,256,1792]{2,1,0:T(8,128)}, f32[8,256,1792]{2,1,0:T(8,128)}) fusion(f32[8,256,1792]{2,1,0:T(8,128)} %get-tuple-element.337, f32[8,256]{1,0:T(8,128)S(1)} %copy-done.29, f32[1792]{0:T(1024)S(1)} %copy-done.35, f32[8,256]{1,0:T(8,128)S(1)} %copy-done.25, f32[1792]{0:T(1024)S(1)} %copy-done.39, ...), kind=kLoop, calls=%fused_computation.50 | loop fusion | flops 22020096 | bytes 58766336 | tf_op jit(solution)/shard_map/transpose(jvp())/mul | solution.py:31
  895.2 22.0 %pad_add_fusion = f32[2048,1792]{1,0:T(8,128)} fusion(f32[2047,1792]{1,0:T(8,128)} %split.14, f32[2046,1792]{1,0:T(8,128)} %split.13, f32[2045,1792]{1,0:T(8,128)} %split.12), kind=kLoop, calls=%fused_computation.43 | loop fusion | flops 7340032 | bytes 58677248 | tf_op jit(solution)/shard_map/transpose(jvp())/add_any | solution.py:24
  917.2 13.3 %multiply_add_fusion = f32[8,256,1792]{2,1,0:T(8,128)} fusion(f32[8,256,1792]{2,1,0:T(8,128)} %bitcast.244, f32[8,256,1792]{2,1,0:T(8,128)S(1)} %bitcast.239, f32[1792]{0:T(1024)S(1)} %copy-done.31), kind=kLoop, calls=%fused_computation.44 | loop fusion | flops 7340032 | bytes 44047360 | tf_op jit(solution)/shard_map/transpose(jvp())/add_any | solution.py:19
  930.8 13.0 %add_convert_fusion = bf16[8,256,3352]{2,1,0:T(8,128)(2,1)} fusion(f32[8,256,1536]{2,1,0:T(8,128)S(1)} %bitcast.249, f32[8,256,1792]{2,1,0:T(8,128)} %multiply_add_fusion, f32[8,256,24]{2,1,0:T(8,128)S(1)} %copy-done.14), kind=kLoop, calls=%fused_computation.23 | loop fusion | flops 20594688 | bytes 41189376 | tf_op jit(solution)/shard_map/convert_element_type | solution.py:180
  943.9 18.0 %fusion.89 = f32[768,3352]{1,0:T(8,128)} fusion(bf16[2048,3352]{1,0:T(8,128)(2,1)} %bitcast.250, bf16[2048,768]{1,0:T(8,128)(2,1)S(1)} %copy-done.5, f32[768]{0:T(1024)S(1)} %copy-done.51, f32[2048]{0:T(1024)S(1)} %copy-done.43), kind=kOutput, calls=%fused_computation.133 | convolution fusion | flops 10550771712 | bytes 27184128 | tf_op jit(solution)/shard_map/dot_general | solution.py:181
  962.3 18.9 %fusion.52 = (f32[768]{0:T(1024)S(1)}, f32[2048]{0:T(1024)S(1)}, f32[2048,768]{1,0:T(8,128)}) fusion(bf16[2048,768]{1,0:T(8,128)(2,1)S(1)} %copy-done.6, f32[2048]{0:T(1024)S(1)} %copy-done.43, f32[768]{0:T(1024)S(1)} %copy-done.51, bf16[2048,3352]{1,0:T(8,128)(2,1)} %bitcast.251, bf16[768,3352]{1,0:T(8,128)(2,1)} %all-gather.4.cloned.1.call-done), kind=kOutput, calls=%fused_computation.94 | convolution fusion | flops 10555487232 | bytes 28338176 | tf_op jit(solution)/shard_map/dot_general | solution.py:184
  981.1 40.6 %all-reduce.26 = (f32[768]{0:T(1024)S(1)}, f32[4,1792]{1,0:T(4,128)S(1)}, f32[1792]{0:T(1024)S(1)}, f32[24]{0:T(128)}, f32[24]{0:T(128)}, /*index=5*/f32[24]{0:T(128)}, f32[1536]{0:T(1024)S(1)}) all-reduce(f32[768]{0:T(1024)S(1)} %get-tuple-element.285, ...), channel_id=2, replica_groups=mesh['dp'=8,'fsdp'=4] {'dp','fsdp'}, use_global_device_ids=true, to_apply=%region_19.20.clone | all-reduce | flops 11336 | bytes 90688
  1039.3 71.6 %reduce-scatter.8.cloned.1.call-done = f32[24,3352]{1,0:T(8,128)} async-done(((f32[768,3352]{1,0:T(8,128)}), f32[24,3352]{1,0:T(8,128)}) %reduce-scatter.8.cloned.1.call-update) | async-done | bytes 321808
  (337 shorter events, 272.0 us)
Async XLA Ops:
  7.2 93.0 %all-gather.6.cloned.1.call-start = ((), (), s32[]{:S(2)}) async-start(), calls=%async_computation.3 | async-start | bytes 2433024 | tf_op jit(solution)/shard_map/all_gather | solution.py:96
  7.9 130.4 %all-gather.4.cloned.1.call-start = ((), (), s32[]{:S(2)}) async-start(), calls=%async_computation.2 | async-start | bytes 5474304 | tf_op jit(solution)/shard_map/all_gather | solution.py:92
  8.7 1030.7 %reduce-scatter.6.cloned.1.call-start = ((), (), s32[]{:S(2)}) async-start(), calls=%async_computation.4 | async-start | bytes 4866048 | tf_op jit(solution)/shard_map/reduce_scatter | solution.py:108
  53.6 84.8 %copy-start.50 = (f32[768]{0:T(1024)}, f32[768]{0:T(1024)S(1)}, u32[]{:S(2)}) copy-start(f32[768]{0:T(1024)S(1)} %convert_element_type.76) | copy-start | bytes 9220
  95.9 528.7 %copy-start.41 = (pred[256,256]{1,0:T(8,128)(4,1)}, pred[256,256]{1,0:T(8,128)(4,1)S(1)}, u32[]{:S(2)}) copy-start(pred[256,256]{1,0:T(8,128)(4,1)S(1)} %iota_compare_fusion) | copy-start | bytes 196612
  96.0 115.0 %copy-start.30 = (f32[1792]{0:T(1024)}, f32[1792]{0:T(1024)S(1)}, u32[]{:S(2)}) copy-start(f32[1792]{0:T(1024)S(1)} %get-tuple-element.287) | copy-start | bytes 21508
  96.0 115.0 %copy-start.34 = (f32[1792]{0:T(1024)}, f32[1792]{0:T(1024)S(1)}, u32[]{:S(2)}) copy-start(f32[1792]{0:T(1024)S(1)} %get-tuple-element.288) | copy-start | bytes 21508
  96.0 115.0 %copy-start.36 = (f32[1792]{0:T(1024)}, f32[1792]{0:T(1024)S(1)}, u32[]{:S(2)}) copy-start(f32[1792]{0:T(1024)S(1)} %get-tuple-element.289) | copy-start | bytes 21508
  96.0 115.0 %copy-start.38 = (f32[1792]{0:T(1024)}, f32[1792]{0:T(1024)S(1)}, u32[]{:S(2)}) copy-start(f32[1792]{0:T(1024)S(1)} %get-tuple-element.290) | copy-start | bytes 21508
  97.3 72.2 %copy-start.57 = (f32[24]{0:T(128)}, f32[24]{0:T(128)S(1)}, u32[]{:S(2)}) copy-start(f32[24]{0:T(128)S(1)} %exponential_negate_fusion) | copy-start | bytes 292
  100.1 38.3 %copy-start.42 = (f32[2048]{0:T(1024)}, f32[2048]{0:T(1024)S(1)}, u32[]{:S(2)}) copy-start(f32[2048]{0:T(1024)S(1)} %fusion.109) | copy-start | bytes 24580
  100.2 110.8 %copy-start.24 = (f32[8,256]{1,0:T(8,128)}, f32[8,256]{1,0:T(8,128)S(1)}, u32[]{:S(2)}) copy-start(f32[8,256]{1,0:T(8,128)S(1)} %get-tuple-element.356) | copy-start | bytes 24580
  100.2 110.8 %copy-start.26 = (f32[8,256]{1,0:T(8,128)}, f32[8,256]{1,0:T(8,128)S(1)}, u32[]{:S(2)}) copy-start(f32[8,256]{1,0:T(8,128)S(1)} %get-tuple-element.357) | copy-start | bytes 24580
  100.2 110.8 %copy-start.28 = (f32[8,256]{1,0:T(8,128)}, f32[8,256]{1,0:T(8,128)S(1)}, u32[]{:S(2)}) copy-start(f32[8,256]{1,0:T(8,128)S(1)} %get-tuple-element.358) | copy-start | bytes 24580
  171.4 97.6 %copy-start.7 = (f32[8,256,24]{2,1,0:T(8,128)}, f32[8,256,24]{2,1,0:T(8,128)S(1)}, u32[]{:S(2)}) copy-start(f32[8,256,24]{2,1,0:T(8,128)S(1)} %get-tuple-element.343) | copy-start | bytes 589828
  176.8 447.8 %copy-start.17 = (f32[8,24,256]{2,1,0:T(8,128)}, f32[8,24,256]{2,1,0:T(8,128)S(1)}, u32[]{:S(2)}) copy-start(f32[8,24,256]{2,1,0:T(8,128)S(1)} %copy_bitcast_fusion) | copy-start | bytes 589828
  354.6 62.4 %copy-start.4 = (f32[8,24,64,256]{3,2,1,0:T(8,128)}, f32[8,24,64,256]{3,2,1,0:T(8,128)S(1)}, u32[]{:S(2)}) copy-start(f32[8,24,64,256]{3,2,1,0:T(8,128)S(1)} %fusion.84) | copy-start | bytes 37748740
  574.0 42.7 %slice-start = ((s8[12582912]{0:T(1024)(128)(4,1)}), s8[4194304]{0:T(1024)(128)(4,1)S(1)}, s32[]{:S(2)}) async-start(s8[12582912]{0:T(1024)(128)(4,1)} %bitcast.228), calls=%async_computation.6 | async-start | bytes 8388608
  574.1 42.7 %slice-start.1 = ((s8[12582912]{0:T(1024)(128)(4,1)}), s8[4194304]{0:T(1024)(128)(4,1)S(1)}, s32[]{:S(2)}) async-start(s8[12582912]{0:T(1024)(128)(4,1)} %bitcast.228), calls=%async_computation.7 | async-start | bytes 8388608
  624.6 73.4 %copy-start.18 = (f32[8,24,1]{2,1,0:T(8,128)S(1)}, f32[8,24,1]{2,1,0:T(8,128)}, u32[]{:S(2)}) copy-start(f32[8,24,1]{2,1,0:T(8,128)} %copy.163) | copy-start | bytes 2308
  624.6 73.4 %copy-start.19 = (f32[8,24,1]{2,1,0:T(8,128)S(1)}, f32[8,24,1]{2,1,0:T(8,128)}, u32[]{:S(2)}) copy-start(f32[8,24,1]{2,1,0:T(8,128)} %copy.162) | copy-start | bytes 2308
  624.6 94.4 %copy-start.62 = (f32[24]{0:T(128)S(1)}, f32[24]{0:T(128)}, u32[]{:S(2)}) copy-start(f32[24]{0:T(128)} %param.24) | copy-start | bytes 292
  718.9 49.5 %copy-start.12 = (f32[8,256,128]{2,1,0:T(8,128)S(1)}, f32[8,256,128]{2,1,0:T(8,128)}, u32[]{:S(2)}) copy-start(f32[8,256,128]{2,1,0:T(8,128)} %fusion.71) | copy-start | bytes 3145732
  718.9 52.7 %copy-start.13 = (f32[8,256,128]{2,1,0:T(8,128)S(1)}, f32[8,256,128]{2,1,0:T(8,128)}, u32[]{:S(2)}) copy-start(f32[8,256,128]{2,1,0:T(8,128)} %fusion.68) | copy-start | bytes 3145732
  790.0 38.1 %copy-start.35 = (f32[1792]{0:T(1024)S(1)}, f32[1792]{0:T(1024)}, u32[]{:S(2)}) copy-start(f32[1792]{0:T(1024)} %copy-done.34) | copy-start | bytes 21508
  790.0 38.1 %copy-start.37 = (f32[1792]{0:T(1024)S(1)}, f32[1792]{0:T(1024)}, u32[]{:S(2)}) copy-start(f32[1792]{0:T(1024)} %copy-done.36) | copy-start | bytes 21508
  790.0 38.1 %copy-start.39 = (f32[1792]{0:T(1024)S(1)}, f32[1792]{0:T(1024)}, u32[]{:S(2)}) copy-start(f32[1792]{0:T(1024)} %copy-done.38) | copy-start | bytes 21508
  856.4 254.5 %reduce-scatter.8.cloned.1.call-start = ((), (), s32[]{:S(2)}) async-start(), calls=%async_computation.5 | async-start | bytes 10948608
  895.2 35.3 %slice-start.7 = ((s8[12582912]{0:T(1024)(128)(4,1)}), s8[4194304]{0:T(1024)(128)(4,1)S(1)}, s32[]{:S(2)}) async-start(s8[12582912]{0:T(1024)(128)(4,1)} %bitcast.248), calls=%async_computation.13 | async-start | bytes 8388608
  895.2 35.3 %slice-start.8 = ((s8[12582912]{0:T(1024)(128)(4,1)}), s8[4194304]{0:T(1024)(128)(4,1)S(1)}, s32[]{:S(2)}) async-start(s8[12582912]{0:T(1024)(128)(4,1)} %bitcast.248), calls=%async_computation.14 | async-start | bytes 8388608
  962.3 61.9 %copy-start.33 = (f32[2048]{0:T(1024)S(1)}, f32[2048]{0:T(1024)}, u32[]{:S(2)}) copy-start(f32[2048]{0:T(1024)} %copy-done.32) | copy-start | bytes 24580
  981.1 48.9 %copy-start.54 = (f32[1,2,8,128]{3,1,2,0:T(2,128)S(1)}, f32[1,2,8,128]{3,1,2,0:T(2,128)}, u32[]{:S(2)}) copy-start(f32[1,2,8,128]{3,1,2,0:T(2,128)} %copy-done.52) | copy-start | bytes 24580
  (46 other events, 696.5 us)
Sparse Core Ops, SparseCore 0:
  10.9 60.0 all-gather.5
  73.9 64.4 all-gather.3
  856.5 105.8 reduce-scatter.5
  969.9 140.9 reduce-scatter.7
where the time goes:
time: 1130 us; the launch traced here: 1120 us
  matrix products  396 us (35%)
  other arithmetic  313 us (28%)
  local copies, waits for them, and re-layouts  169 us (15%)
  blocking collectives  124 us (11%)
  waiting for transfers between devices  100 us (9%)
  between operations  15 us (1%)
    dot_general x3, matrix products, span_scan(): inside = jnp.einsum('chij,cjhp->cihp', mixing, weighted, precision=precise)  185 us
    unnamed x2, blocking collectives  82.8 us
    unnamed x5, waiting for transfers between devices  73 us
    dot_general x3, matrix products, span_scan(): jnp.einsum('chj,cjn,cjhp->chpn', leaving, into_state, weighted, precision...  59.2 us
    dot_general x3, matrix products, span_scan(): jnp.einsum('cin,chpn,chi->cihp', read_state, entering, jnp.exp(running),...  52.5 us
    all_gather x1, blocking collectives, collect(): lax.all_gather(conv_taps, ('dp', 'fsdp'), axis=1, tiled=True)  40.8 us
    reduce_sum x1, other arithmetic, causal_conv(): conv_shift[None, None, :] + conv_taps[tap_count - 1][None, None, :] * signal  38.1 us
    split x3, local copies, waits for them, and re-layouts, causal_conv(): jnp.concatenate([jnp.zeros((shift_by, width), jnp.float32), flat[:-shift_...  35 us
  transfers between devices with their start and end apart: 4, of which 2 were waited for; matrix products, arithmetic and copies ran while one was open for 14% of the time, Pallas kernels for 0%

commit v1 on v0

v1 whole, which is shorter than its diff:
```python
import jax
import jax.numpy as jnp
from jax import lax
from jax.experimental import pallas as pl
from jax.experimental.pallas import tpu as pltpu
from jax.sharding import PartitionSpec as P

epsilon = 1e-05
f32 = jnp.float32
bf16 = jnp.bfloat16
Q = 128
PAD = 128
AXES = ("dp", "fsdp")


def mm(a, b, ca=1, cb=0):
    return lax.dot_general(a, b, (((ca,), (cb,)), ((), ())), preferred_element_type=f32)


def split2(v):
    hi = v.astype(bf16)
    return hi, (v - hi.astype(f32)).astype(bf16)


def spread_heads(v, heads_map):
    hi, lo = split2(v)
    return mm(hi, heads_map) + mm(lo, heads_map)


def sum_heads(v, heads_map):
    hi, lo = split2(v)
    return mm(hi, heads_map, 1, 1) + mm(lo, heads_map, 1, 1)


def tri_sum(tri, v):
    hi = v.astype(bf16)
    rest = v - hi.astype(f32)
    mid = rest.astype(bf16)
    low = (rest - mid.astype(f32)).astype(bf16)
    return mm(tri, hi) + mm(tri, mid) + mm(tri, low)


def sigmoid(v):
    return 1.0 / (1.0 + jnp.exp(-v))


def softplus(v):
    return jnp.maximum(v, 0.0) + jnp.log1p(jnp.exp(-jnp.abs(v)))


def forward_kernel(
    start_ref, tokens_ref, bgrad_ref, w_ref, wstep_ref, wout_ref, gain_ref, taps_ref, bias_ref,
    rates_ref, sbias_ref, skip_ref, ggain_ref, map_ref,
    normed_ref, gated_ref, dgate_ref, dy_ref, rs_ref, pre_ref, cpart_ref, sraw_ref, state_out_ref,
    ggrad_ref, skipgrad_ref,
    ext, state, ybuf,
):
    inner = ggain_ref.shape[1]
    chans = bias_ref.shape[1]
    nstate = (chans - inner) // 2
    pairs = inner // 128
    step = pl.program_id(0)
    per = pl.num_programs(0) // start_ref.shape[0]
    fresh = jnp.logical_and(step % per == 0, start_ref[step // per] == 1)

    @pl.when(step == 0)
    def _():
        ggrad_ref[...] = jnp.zeros_like(ggrad_ref)
        skipgrad_ref[...] = jnp.zeros_like(skipgrad_ref)

    @pl.when(jnp.logical_or(fresh, step == 0))
    def _():
        state[...] = jnp.zeros_like(state)
        ext[0:8, :] = jnp.zeros((8, chans), f32)

    rows = tokens_ref[...].astype(f32)
    r = lax.rsqrt(jnp.mean(rows * rows, axis=1, keepdims=True) + epsilon)
    normed = (rows * r * gain_ref[...]).astype(bf16)
    normed_ref[...] = normed
    heads_map = map_ref[...]
    cpart = mm(normed, w_ref[:, inner : inner + chans])
    cpart_ref[...] = cpart.astype(bf16)
    ext[8:, :] = cpart
    pre = bias_ref[...] + taps_ref[3:4, :] * cpart
    for j in range(3):
        pre = pre + taps_ref[j : j + 1, :] * ext[5 + j : 5 + j + Q, :]
    ext[0:8, :] = ext[Q : Q + 8, :]
    pre_ref[...] = pre
    conv = pre * sigmoid(pre)
    x = conv[:, :inner]
    b = conv[:, inner : inner + nstate]
    c = conv[:, inner + nstate :]
    b16 = b.astype(bf16)
    c16 = c.astype(bf16)
    sraw = mm(normed, wstep_ref[...]) + sbias_ref[...]
    sraw_ref[...] = sraw
    dt = softplus(sraw)
    ri = lax.broadcasted_iota(jnp.int32, (Q, Q), 0)
    ci = lax.broadcasted_iota(jnp.int32, (Q, Q), 1)
    lower = ri >= ci
    run = tri_sum(jnp.where(lower, 1.0, 0.0).astype(bf16), dt * rates_ref[...])
    run_t = run.T
    w = x * spread_heads(dt, heads_map)
    w16 = w.astype(bf16)
    er = spread_heads(jnp.exp(run), heads_map)
    leaving = spread_heads(jnp.exp(run[Q - 1 : Q, :] - run), heads_map)
    lw16 = (leaving * w16.astype(f32)).astype(bf16)
    inter = mm(c16, b16, 1, 1)
    left = lax.broadcasted_iota(jnp.int32, (Q, 128), 1) < 64
    zero16 = jnp.zeros((Q, 128), bf16)
    state16 = state[...].astype(bf16)
    state_out_ref[0] = state16
    ybuf[...] = mm(c16, state16) * er
    for k in range(pairs):
        mats = []
        for h in (2 * k, 2 * k + 1):
            seg = run[:, h : h + 1] - run_t[h : h + 1, :]
            e = jnp.exp(jnp.where(lower, seg, -1e30))
            mats.append((e * inter).astype(bf16))
        wp = w16[:, 128 * k : 128 * k + 128]
        rhs = jnp.concatenate([jnp.where(left, wp, zero16), jnp.where(left, zero16, wp)], axis=0)
        ybuf[:, 128 * k : 128 * k + 128] += mm(jnp.concatenate(mats, axis=1), rhs)
    state[...] = er[Q - 1 : Q, :] * state[...] + mm(b.T.astype(bf16), lw16)

    y = ybuf[...]
    gate = mm(normed, w_ref[:, :inner])
    ggrad = mm(bgrad_ref[...], wout_ref[...], 1, 1)
    scanned = y + skip_ref[...] * x
    sg = sigmoid(gate)
    sil = gate * sg
    m = scanned * sil
    r2 = lax.rsqrt(jnp.mean(m * m, axis=1, keepdims=True) + epsilon)
    u = m * r2
    gated_ref[...] = (u * ggain_ref[...]).astype(bf16)
    ggrad_ref[...] += jnp.sum(ggrad * u, axis=0, keepdims=True)
    g = ggrad * ggain_ref[...]
    dm = r2 * (g - u * jnp.mean(g * u, axis=1, keepdims=True))
    dgate_ref[...] = (dm * scanned * (sg * (1.0 + gate * (1.0 - sg)))).astype(bf16)
    dsc = dm * sil
    skipgrad_ref[...] += jnp.sum(dsc * x, axis=0, keepdims=True)
    dy16 = dsc.astype(bf16)
    dy_ref[...] = dy16
    rs_ref[...] = sum_heads(dy16.astype(f32) * y, heads_map)


def backward_kernel(
    start_ref, dy_ref, rs_ref, pre_ref, cpart_ref, sraw_ref, state_in_ref, taps_ref, rates_ref,
    skip_ref, map_ref,
    dcs_ref, dtaps_ref, dbias_ref, ddecay_ref, dstep_ref,
    ext, dstate, dwbuf,
):
    inner = skip_ref.shape[1]
    chans = taps_ref.shape[1]
    nstate = (chans - inner) // 2
    pairs = inner // 128
    heads = dcs_ref.shape[1] - chans
    step = pl.program_id(0)
    steps = pl.num_programs(0)
    at = steps - 1 - step
    per = steps // start_ref.shape[0]
    fresh = jnp.logical_and(at % per == 0, start_ref[at // per] == 1)

    @pl.when(step == 0)
    def _():
        dtaps_ref[...] = jnp.zeros_like(dtaps_ref)
        dbias_ref[...] = jnp.zeros_like(dbias_ref)
        ddecay_ref[...] = jnp.zeros_like(ddecay_ref)
        dstep_ref[...] = jnp.zeros_like(dstep_ref)
        dstate[...] = jnp.zeros_like(dstate)
        ext[Q:, :] = jnp.zeros((8, chans), f32)

    heads_map = map_ref[...]
    pre = pre_ref[...]
    sgm = sigmoid(pre)
    conv = pre * sgm
    x = conv[:, :inner]
    b = conv[:, inner : inner + nstate]
    c = conv[:, inner + nstate :]
    b16 = b.astype(bf16)
    c16 = c.astype(bf16)
    sraw = sraw_ref[...]
    dt = softplus(sraw)
    rates = rates_ref[...]
    ri = lax.broadcasted_iota(jnp.int32, (Q, Q), 0)
    ci = lax.broadcasted_iota(jnp.int32, (Q, Q), 1)
    upper = ci >= ri
    run = tri_sum(jnp.where(ri >= ci, 1.0, 0.0).astype(bf16), dt * rates)
    run_t = run.T
    dt_e = spread_heads(dt, heads_map)
    w16 = (x * dt_e).astype(bf16)
    wf = w16.astype(f32)
    er = spread_heads(jnp.exp(run), heads_map)
    leaving = spread_heads(jnp.exp(run[Q - 1 : Q, :] - run), heads_map)
    lw16 = (leaving * wf).astype(bf16)
    inter_t = mm(b16, c16, 1, 1)
    dy16 = dy_ref[...]
    dy = dy16.astype(f32)
    ds = dstate[...]
    ds16 = ds.astype(bf16)
    s16 = state_in_ref[0]
    left = lax.broadcasted_iota(jnp.int32, (Q, 128), 1) < 64
    zero16 = jnp.zeros((Q, 128), bf16)
    dinter_t = jnp.zeros((Q, Q), f32)
    for k in range(pairs):
        wp = w16[:, 128 * k : 128 * k + 128]
        dyp = dy16[:, 128 * k : 128 * k + 128]
        both_w = jnp.concatenate([jnp.where(left, wp, zero16), jnp.where(left, zero16, wp)], axis=0)
        dmt = mm(both_w, dyp, 1, 1)
        mats = []
        for n in range(2):
            h = 2 * k + n
            seg = run_t[h : h + 1, :] - run[:, h : h + 1]
            e = jnp.exp(jnp.where(upper, seg, -1e30))
            mats.append((e * inter_t).astype(bf16))
            dinter_t = dinter_t + dmt[n * Q : n * Q + Q, :] * e
        rhs = jnp.concatenate([jnp.where(left, dyp, zero16), jnp.where(left, zero16, dyp)], axis=0)
        dwbuf[:, 128 * k : 128 * k + 128] = mm(jnp.concatenate(mats, axis=1), rhs)
    dey16 = (dy * er).astype(bf16)
    dep = leaving * mm(b16, ds16)
    dw = dwbuf[...] + dep
    db = mm(dinter_t.astype(bf16), c16) + mm(lw16, ds16, 1, 1)
    dc = mm(dinter_t.T.astype(bf16), b16) + mm(dey16, s16, 1, 1)
    carried = er[Q - 1 : Q, :]
    end = jnp.sum(wf * dep, axis=0, keepdims=True) + carried * jnp.sum(
        s16.astype(f32) * ds, axis=0, keepdims=True
    )
    end = sum_heads(jnp.broadcast_to(end, (8, inner)), heads_map)[0:1, :]
    keep = jnp.where(fresh, 0.0, 1.0)
    dstate[...] = (carried * ds + mm(c.T.astype(bf16), dey16)) * keep
    drun = rs_ref[...] - sum_heads(wf * dw, heads_map)
    da = tri_sum(jnp.where(upper, 1.0, 0.0).astype(bf16), drun) + end
    ddt = da * rates + sum_heads(dw * x, heads_map)
    ddecay_ref[...] += jnp.sum(da * dt * rates, axis=0, keepdims=True)
    dsr = ddt * sigmoid(sraw)
    dstep_ref[...] += jnp.sum(dsr, axis=0, keepdims=True)
    dcs_ref[:, chans:] = dsr[:, :heads].astype(bf16)
    dx = dw * dt_e + skip_ref[...] * dy
    dsilu = sgm * (1.0 + pre * (1.0 - sgm))
    ext[0:Q, :inner] = dx * dsilu[:, :inner]
    ext[0:Q, inner : inner + nstate] = db * dsilu[:, inner : inner + nstate]
    ext[0:Q, inner + nstate :] = dc * dsilu[:, inner + nstate :]
    cpart = cpart_ref[...].astype(f32)
    dcp = jnp.zeros((Q, chans), f32)
    for s in range(4):
        moved = ext[s : s + Q, :]
        if s == 0:
            dbias_ref[...] += jnp.sum(moved, axis=0, keepdims=True)
        dcp = dcp + taps_ref[3 - s : 4 - s, :] * moved
        dtaps_ref[3 - s : 4 - s, :] += jnp.sum(cpart * moved, axis=0, keepdims=True)
    dcs_ref[:, :chans] = dcp.astype(bf16)
    ext[Q:, :] = ext[0:8, :] * keep


def whole(shape):
    return pl.BlockSpec(shape, lambda i: (0,) * len(shape))


def run_forward(start, tokens, bgrad, w, wstep, wout, gain, taps, bias, rates, sbias, skip, ggain, heads_map):
    count, width = tokens.shape
    inner = ggain.shape[1]
    chans = bias.shape[1]
    nstate = (chans - inner) // 2
    steps = count // Q

    def rowblock(n):
        return pl.BlockSpec((Q, n), lambda i: (i, 0))

    consts = (w, wstep, wout, gain, taps, bias, rates, sbias, skip, ggain, heads_map)
    sds = jax.ShapeDtypeStruct
    return pl.pallas_call(
        forward_kernel,
        grid=(steps,),
        in_specs=[pl.BlockSpec(memory_space=pltpu.SMEM), rowblock(width), rowblock(width)]
        + [whole(v.shape) for v in consts],
        out_specs=[
            rowblock(width), rowblock(inner), rowblock(inner), rowblock(inner), rowblock(PAD),
            rowblock(chans), rowblock(chans), rowblock(PAD),
            pl.BlockSpec((1, nstate, inner), lambda i: (i, 0, 0)),
            whole((1, inner)), whole((1, inner)),
        ],
        out_shape=[
            sds((count, width), bf16), sds((count, inner), bf16), sds((count, inner), bf16),
            sds((count, inner), bf16), sds((count, PAD), f32), sds((count, chans), f32),
            sds((count, chans), bf16), sds((count, PAD), f32), sds((steps, nstate, inner), bf16),
            sds((1, inner), f32), sds((1, inner), f32),
        ],
        scratch_shapes=[
            pltpu.VMEM((Q + 8, chans), f32), pltpu.VMEM((nstate, inner), f32), pltpu.VMEM((Q, inner), f32),
        ],
        compiler_params=pltpu.CompilerParams(
            dimension_semantics=("arbitrary",), vmem_limit_bytes=56 * 1024 * 1024
        ),
        cost_estimate=pl.CostEstimate(flops=30_000_000_000, bytes_accessed=80_000_000, transcendentals=20_000_000),
        name="mixer_forward",
    )(start, tokens, bgrad, *consts)


def run_backward(start, dy, rs, pre, cpart, sraw, states, taps, rates, skip, heads_map, heads):
    count, inner = dy.shape
    chans = pre.shape[1]
    nstate = states.shape[1]
    steps = count // Q

    def rowblock(n):
        return pl.BlockSpec((Q, n), lambda i: (steps - 1 - i, 0))

    consts = (taps, rates, skip, heads_map)
    sds = jax.ShapeDtypeStruct
    return pl.pallas_call(
        backward_kernel,
        grid=(steps,),
        in_specs=[
            pl.BlockSpec(memory_space=pltpu.SMEM), rowblock(inner), rowblock(PAD), rowblock(chans),
            rowblock(chans), rowblock(PAD),
            pl.BlockSpec((1, nstate, inner), lambda i: (steps - 1 - i, 0, 0)),
        ]
        + [whole(v.shape) for v in consts],
        out_specs=[
            rowblock(chans + heads), whole((4, chans)), whole((1, chans)), whole((1, PAD)), whole((1, PAD)),
        ],
        out_shape=[
            sds((count, chans + heads), bf16), sds((4, chans), f32), sds((1, chans), f32),
            sds((1, PAD), f32), sds((1, PAD), f32),
        ],
        scratch_shapes=[
            pltpu.VMEM((Q + 8, chans), f32), pltpu.VMEM((nstate, inner), f32), pltpu.VMEM((Q, inner), f32),
        ],
        compiler_params=pltpu.CompilerParams(
            dimension_semantics=("arbitrary",), vmem_limit_bytes=56 * 1024 * 1024
        ),
        cost_estimate=pl.CostEstimate(flops=30_000_000_000, bytes_accessed=60_000_000, transcendentals=20_000_000),
        name="mixer_backward",
    )(start, dy, rs, pre, cpart, sraw, states, *consts)


def local_mixer(tokens, bgrad, w, wout, gain, taps, bias, decay_log, step_bias, skip_gain, ggain, start):
    inner = ggain.shape[0]
    chans = bias.shape[0]
    heads = decay_log.shape[0]
    lane = jnp.arange(inner, dtype=jnp.int32) // (inner // heads)
    heads_map = (jnp.arange(PAD, dtype=jnp.int32)[:, None] == lane[None, :]).astype(bf16)

    def padded(v):
        return jnp.pad(v, (0, PAD - heads))[None, :]

    rates = padded(-jnp.exp(decay_log))
    skip = jnp.repeat(skip_gain, inner // heads)[None, :]
    wstep = jnp.pad(w[:, inner + chans : inner + chans + heads], ((0, 0), (0, PAD - heads)))
    taps = taps.astype(f32)
    bias = bias.astype(f32)[None, :]
    normed, gated, dgate, dy, rs, pre, cpart, sraw, states, ggrad, skipgrad = run_forward(
        start, tokens, bgrad, w, wstep, wout, gain.astype(f32)[None, :], taps, bias, rates,
        padded(step_bias), skip, ggain.astype(f32)[None, :], heads_map,
    )
    dcs, dtaps, dbias, ddecay, dstep = run_backward(
        start, dy, rs, pre, cpart, sraw, states, taps, rates, skip, heads_map, heads
    )
    skip_grad = skipgrad.reshape(heads, -1).sum(axis=1)
    return normed, gated, dgate, dcs, dtaps, dbias[0], ddecay[0, :heads], dstep[0, :heads], skip_grad, ggrad[0]


def per_device(
    tokens, norm_gain, in_weight, conv_weight, conv_bias, decay_log, step_bias, skip_gain, gate_gain,
    out_weight, span_start, span_valid, cotangent,
):
    spans = span_start.shape[0]
    length = tokens.shape[0] // spans
    offsets = jnp.arange(length, dtype=jnp.int32)
    live = (offsets[None, :] < span_valid[:, None]).astype(f32).reshape(-1, 1)
    wrows, proj = in_weight.shape
    smalls = [norm_gain, conv_weight.reshape(-1), conv_bias, gate_gain]
    total = sum(v.shape[0] for v in smalls)
    extra = -(-total // wrows)
    extra = -(-extra // 8) * 8
    flat = jnp.concatenate(smalls + [jnp.zeros((extra * wrows - total,), bf16)])
    joined = jnp.concatenate([in_weight, flat.reshape(wrows, extra)], axis=1)
    full_w = lax.all_gather(joined, AXES, axis=0, tiled=True)
    full_out = lax.all_gather(out_weight, AXES, axis=0, tiled=True)
    small = full_w[:, proj:].reshape(-1, extra * wrows)
    edges = [0]
    for v in smalls:
        edges.append(edges[-1] + v.shape[0])
    full_norm = small[:, edges[0] : edges[1]].reshape(-1)
    devices = small.shape[0]
    full_taps = small[:, edges[1] : edges[2]].reshape(devices, conv_weight.shape[0], -1)
    full_taps = full_taps.transpose(1, 0, 2).reshape(conv_weight.shape[0], -1)
    full_bias = small[:, edges[2] : edges[3]].reshape(-1)
    full_gate = small[:, edges[3] : edges[4]].reshape(-1)
    inner = full_gate.shape[0]

    flowing = cotangent.astype(f32)
    branch_grad = (flowing * live).astype(bf16)
    (normed, gated, dgate, dcs, taps_grad, bias_grad, decay_grad, step_grad, skip_grad, gain_grad) = local_mixer(
        tokens, branch_grad, full_w, full_out, full_norm, full_taps, full_bias, decay_log, step_bias,
        skip_gain, full_gate, span_start,
    )
    scatter = lambda v, dim=0: lax.psum_scatter(v, AXES, scatter_dimension=dim, tiled=True)
    out_share = scatter(mm(gated, branch_grad, 0, 0))
    gate_share = scatter(mm(normed, dgate, 0, 0))
    rest_share = scatter(mm(normed, dcs, 0, 0))
    normed_grad = mm(dgate, full_w[:, :inner], 1, 1) + mm(dcs, full_w[:, inner:proj], 1, 1)
    rows = tokens.astype(f32)
    r = lax.rsqrt(jnp.mean(rows * rows, axis=1, keepdims=True) + epsilon)
    u = rows * r
    norm_grad = jnp.sum(normed_grad * u, axis=0)
    g = normed_grad * full_norm.astype(f32)[None, :]
    token_grad = (flowing + r * (g - u * jnp.mean(g * u, axis=1, keepdims=True))).astype(bf16)
    branch = mm(gated, full_out)
    output = (rows + branch * live).astype(bf16)
    head_sums = lax.psum((decay_grad, step_grad, skip_grad), AXES)
    return (
        output,
        token_grad,
        scatter(norm_grad),
        jnp.concatenate([gate_share, rest_share], axis=1),
        scatter(taps_grad, 1),
        scatter(bias_grad),
        head_sums[0],
        head_sums[1],
        head_sums[2],
        scatter(gain_grad),
        out_share,
    )


def solution(mesh):
    rows = P(AXES, None)
    vec = P(AXES)
    cols = P(None, AXES)
    in_specs = (rows, vec, rows, cols, vec, P(), P(), P(), vec, rows, vec, vec, rows)
    out_specs = (rows, rows, vec, rows, cols, vec, P(), P(), P(), vec, rows)
    return jax.shard_map(
        per_device, mesh=mesh, in_specs=in_specs, out_specs=out_specs, check_vma=False
    )
```

time: 1130 us -> 567 us (0.50); the launches traced: 1120 us -> 567 us
  matrix products: 396 us -> 60 us
  other arithmetic: 313 us -> 16.9 us
  waiting for transfers between devices: 100 us -> 276 us
  local copies, waits for them, and re-layouts: 169 us -> 16.3 us
  Pallas kernels: 0 us -> 143 us
  blocking collectives: 124 us -> 39.5 us
    dot_general x17 -> x6, matrix products: 376 us -> 60 us  [mm(): lax.dot_general(a, b, (((ca,), (cb,)), ((), ())), preferred_element_type=...]
    pallas_call x0 -> x2, Pallas kernels: none -> 143 us  [the longest x1 73.4 us: run_forward(): pl.pallas_call(forward_kernel, grid=(steps,), in_specs=[pl.BlockSpec(memo...]
    reduce_sum x16 -> x2, other arithmetic: 120 us -> 0.8 us  [the longest x1 0.68 us: per_device(): r = lax.rsqrt(jnp.mean(rows * rows, axis=1, keepdims=True) + epsilon)]
    reduce_scatter x1 -> x2, waiting for transfers between devices: 0.01 us -> 111 us  [per_device(): lax.psum_scatter(v, AXES, scatter_dimension=dim, tiled=True)]
    all_gather x2, waiting for transfers between devices: 27.5 us -> 112 us  [the longest x1 58.7 us: per_device(): full_w = lax.all_gather(joined, AXES, axis=0, tiled=True)]
    mul x4 -> x0, other arithmetic: 51.5 us -> none  [the longest x1 30.3 us: mixer(): jax.nn.silu(causal_conv(conv_part, conv_taps, conv_shift, span_start))]
    unnamed x2 -> x1, blocking collectives: 82.8 us -> 39.5 us
    all_gather x1 -> x0, blocking collectives: 40.8 us -> none  [collect(): lax.all_gather(conv_taps, ('dp', 'fsdp'), axis=1, tiled=True)]
  transfers between devices with their start and end apart: 4 -> 5, of which waited for: 2 -> 4; matrix products, arithmetic and copies ran while one was open for 14% -> 13% of each run, Pallas kernels for 0% -> 12%
where the time goes in v1:
time: 567 us
  waiting for transfers between devices  276 us (49%)
  Pallas kernels  143 us (25%)
  matrix products  60 us (11%)
  blocking collectives  39.5 us (7%)
  other arithmetic  16.9 us (3%)
  local copies, waits for them, and re-layouts  16.3 us (3%)
  between operations  14 us (2%)
    reduce_scatter x2, waiting for transfers between devices, per_device(): lax.psum_scatter(v, AXES, scatter_dimension=dim, tiled=True)  111 us
    pallas_call x1, Pallas kernels, run_forward(): pl.pallas_call(forward_kernel, grid=(steps,), in_specs=[pl.BlockSpec(memo...  73.4 us
    pallas_call x1, Pallas kernels, run_backward(): pl.pallas_call(backward_kernel, grid=(steps,), in_specs=[pl.BlockSpec(mem...  69.9 us
    dot_general x6, matrix products, mm(): lax.dot_general(a, b, (((ca,), (cb,)), ((), ())), preferred_element_type=...  60 us
    all_gather x1, waiting for transfers between devices, per_device(): full_w = lax.all_gather(joined, AXES, axis=0, tiled=True)  58.7 us
    all_gather x1, waiting for transfers between devices, per_device(): full_out = lax.all_gather(out_weight, AXES, axis=0, tiled=True)  53.1 us
    unnamed x6, waiting for transfers between devices  52.9 us
    unnamed x1, blocking collectives  39.5 us
  transfers between devices with their start and end apart: 5, of which 4 were waited for; matrix products, arithmetic and copies ran while one was open for 13% of the time, Pallas kernels for 12%

profile of v1, /device:TPU:0, one launch (start us, length us, event | category | flops | bytes accessed | tf_op | source)
XLA Modules:
  0.0 566.6 jit_solution(14044348884504012451)
XLA Ops:
  7.2 0.8 reshape.126
  8.0 2.1 concatenate.9
  10.2 1.7 pad_maximum_fusion.1
  11.9 0.7 all-gather.5.cloned.1.call-update
  12.7 0.7 convert_bitcast_fusion
  13.4 0.7 broadcast_in_dim.11
  15.5 1.2 pad_bitcast_fusion
  16.6 0.8 fusion.14.map_ref
  17.5 4.1 fusion.3.bgrad_ref
  21.6 58.7 %all-gather.3.cloned.1.call-done.w_ref = bf16[768,3368]{1,0:T(8,128)(2,1)} async-done(((bf16[24,3368]{1,0:T(8,128)(2,1)}), bf16[768,3368]{1,0:T(8,128)(2,1)}) %all-gather.3.cloned.1.call-update) | async-done | bytes 5173264 | tf_op jit(solution)/shard_map/all_gather | solution.py:377
  80.3 1.0 slice.41
  82.3 0.7 reshape.134.ggain_ref
  83.1 0.7 reshape.133.bias_ref
  84.0 0.7 reshape.132.taps_ref
  84.7 0.9 slice.40
  85.6 0.7 pad.11.wstep_ref
  86.3 53.1 %all-gather.5.cloned.1.call-done.wout_ref = bf16[1536,768]{1,0:T(8,128)(2,1)} async-done(((bf16[48,768]{1,0:T(8,128)(2,1)}), bf16[1536,768]{1,0:T(8,128)(2,1)}) %all-gather.5.cloned.1.call-update) | async-done | bytes 2359312 | tf_op jit(solution)/shard_map/all_gather | solution.py:378
  139.4 73.4 %mixer_forward.1 = (bf16[2048,768]{1,0:T(8,128)(2,1)}, bf16[2048,1536]{1,0:T(8,128)(2,1)}, bf16[2048,1536]{1,0:T(8,128)(2,1)}, bf16[2048,1536]{1,0:T(8,128)(2,1)...) custom-call(s32[8]{0:T(128)} %start_ref.3, ...), custom_call_target="tpu_custom_call" | custom-call | flops 30000001024 | bytes 80000000 | tf_op jit(solution)/shard_map/mixer_forward/pallas_call | solution.py:270
  212.8 9.7 %fusion.18 = f32[768,1536]{1,0:T(8,128)} fusion(bf16[2048,768]{1,0:T(8,128)(2,1)} %get-tuple-element.36, bf16[2048,1536]{1,0:T(8,128)(2,1)} %get-tuple-element.28), kind=kOutput, calls=%fused_computation.45 | convolution fusion | flops 4831838208 | bytes 14155776 | tf_op jit(solution)/shard_map/dot_general | solution.py:17
  222.8 69.9 %mixer_backward.1 = (bf16[2048,1816]{1,0:T(8,128)(2,1)}, f32[4,1792]{1,0:T(4,128)}, f32[1,1792]{1,0:T(1,128)}, f32[1,128]{1,0:T(1,128)}, f32[1,128]{1,0:T(1,128)}) custom-call(s32[8]{0:T(128)} %start_ref.3, bf16[2048,1536]{1,0:T(8,128)(2,1)} %get-tuple-element.29.dy_ref, f32[2048,128]{1,0:T(8,128)} %get-tuple-element.30.rs_ref, ...), custom_call_target="tpu_custom_call" | custom-call | flops 30000001024 | bytes 60000000 | tf_op jit(solution)/shard_map/mixer_backward/pallas_call | solution.py:309
  292.7 10.8 %fusion.19 = f32[768,1816]{1,0:T(8,128)} fusion(bf16[2048,768]{1,0:T(8,128)(2,1)S(1)} %copy-done.11, bf16[2048,1816]{1,0:T(8,128)(2,1)} %get-tuple-element.35), kind=kOutput, calls=%fused_computation.46 | convolution fusion | flops 5712642048 | bytes 16162816 | tf_op jit(solution)/shard_map/dot_general | solution.py:17
  303.8 1.6 copy-done.1
  306.5 9.7 %fusion.20 = f32[1536,768]{1,0:T(8,128)} fusion(bf16[2048,1536]{1,0:T(8,128)(2,1)} %get-tuple-element.27, bf16[2048,768]{1,0:T(8,128)(2,1)} %fusion.3.bgrad_ref), kind=kOutput, calls=%fused_computation.47 | convolution fusion | flops 4831838208 | bytes 14155776 | tf_op jit(solution)/shard_map/dot_general | solution.py:17
  316.3 8.1 %fusion.12 = f32[2048,768]{1,0:T(8,128)S(1)} fusion(bf16[2048,1536]{1,0:T(8,128)(2,1)} %get-tuple-element.28, bf16[768,3368]{1,0:T(8,128)(2,1)} %all-gather.3.cloned.1.call-done.w_ref), kind=kOutput, calls=%fused_computation.18 | convolution fusion | flops 4831838208 | bytes 14942208 | tf_op jit(solution)/shard_map/dot_general | solution.py:17
  324.4 12.5 %fusion.8 = (f32[768]{0:T(1024)S(1)}, f32[2048]{0:T(1024)S(1)}, f32[2048,768]{1,0:T(8,128)}) fusion(bf16[2048,768]{1,0:T(8,128)(2,1)S(1)} %copy-done.2, f32[2048]{0:T(1024)S(1)} %add_rsqrt_fusion, f32[768]{0:T(1024)S(1)} %reshape.135, f32[2048,768]{1,0:T(8,128)S(1)} %fusion.12, bf16[2048,1816]{1,0:T(8,128)(2,1)} %get-tuple-element.35, ...), kind=kOutput, calls=%fused_computation.13 | convolution fusion | flops 5725221888 | bytes 26564608 | tf_op jit(solution)/shard_map/dot_general | solution.py:17
  336.9 39.5 %all-reduce.8 = (f32[768]{0:T(1024)S(1)}, f32[4,1792]{1,0:T(4,128)S(1)}, f32[1792]{0:T(1024)S(1)}, f32[24]{0:T(128)}, f32[24]{0:T(128)}, /*index=5*/f32[24]{0:T(128)}, f32[1536]{0:T(1024)S(1)}) all-reduce(f32[768]{0:T(1024)S(1)} %get-tuple-element.43, ...), channel_id=2, replica_groups=mesh['dp'=8,'fsdp'=4] {'dp','fsdp'}, use_global_device_ids=true, to_apply=%region_3.4.clone | all-reduce | flops 11336 | bytes 90688
  378.8 6.0 %fusion.4 = bf16[2048,768]{1,0:T(8,128)(2,1)} fusion(bf16[2048,768]{1,0:T(8,128)(2,1)S(1)} %copy-done, bf16[2048,768]{1,0:T(8,128)(2,1)} %tokens_ref.1, f32[2048,768]{1,0:T(8,128)} %get-tuple-element.52, f32[2048]{0:T(1024)S(1)} %broadcast_multiply_fusion, f32[768]{0:T(1024)S(1)} %reshape.135, f32[2048]{0:T(1024)S(1)} %add_rsqrt_fusion), kind=kLoop, calls=%fused_computation.9 | loop fusion | flops 14155776 | bytes 15748096 | tf_op jit(solution)/shard_map/convert_element_type | solution.py:407
  384.8 0.8 copy-done.8
  385.7 9.3 %fusion.9 = bf16[2048,768]{1,0:T(8,128)(2,1)} fusion(bf16[2048,768]{1,0:T(8,128)(2,1)S(1)} %copy-done.3, bf16[2048,1536]{1,0:T(8,128)(2,1)} %get-tuple-element.27, bf16[1536,768]{1,0:T(8,128)(2,1)S(1)} %copy-done.8, f32[2048]{0:T(1024)S(1)} %bitcast.26), kind=kOutput, calls=%fused_computation.14 | convolution fusion | flops 4838129664 | bytes 14950400 | tf_op jit(solution)/shard_map/dot_general | solution.py:17
  395.0 52.1 %reduce-scatter.11.cloned.1.call-done = f32[24,1816]{1,0:T(8,128)} async-done(((f32[768,1816]{1,0:T(8,128)}), f32[24,1816]{1,0:T(8,128)}) %reduce-scatter.11.cloned.1.call-update) | async-done | bytes 174352
  447.1 1.7 pad_maximum_fusion
  448.8 111.3 %reduce-scatter.9.cloned.1.call-done = f32[48,768]{1,0:T(8,128)} async-done(((f32[1536,768]{1,0:T(8,128)}), f32[48,768]{1,0:T(8,128)}) %reduce-scatter.9.cloned.1.call-update) | async-done | bytes 147472 | tf_op jit(solution)/shard_map/reduce_scatter | solution.py:397
  (61 shorter events, 6.8 us)
Async XLA Ops:
  7.2 73.2 %all-gather.3.cloned.1.call-start = ((), (), s32[]{:S(2)}) async-start(), calls=%async_computation.3 | async-start | bytes 5474304 | tf_op jit(solution)/shard_map/all_gather | solution.py:377
  11.9 127.6 %all-gather.5.cloned.1.call-start = ((), (), s32[]{:S(2)}) async-start(), calls=%async_computation.4 | async-start | bytes 2433024 | tf_op jit(solution)/shard_map/all_gather | solution.py:378
  12.6 382.3 %reduce-scatter.7.cloned.1.call-start = ((), (), s32[]{:S(2)}) async-start(), calls=%async_computation.5 | async-start | bytes 4866048 | tf_op jit(solution)/shard_map/reduce_scatter | solution.py:397
  222.5 224.5 %reduce-scatter.11.cloned.1.call-start = ((), (), s32[]{:S(2)}) async-start(), calls=%async_computation.7 | async-start | bytes 6082560
  222.8 69.9 %copy-start.11 = (bf16[2048,768]{1,0:T(8,128)(2,1)S(1)}, bf16[2048,768]{1,0:T(8,128)(2,1)}, u32[]{:S(2)}) copy-start(bf16[2048,768]{1,0:T(8,128)(2,1)} %get-tuple-element.36) | copy-start | bytes 9437188
  303.5 1.9 copy-start.1
  303.5 2.7 copy-start.5
  303.5 2.7 copy-start.7
  303.5 2.8 copy-start.6
  303.5 3.0 copy-start.10
  303.5 3.0 copy-start.9
  303.6 256.5 %reduce-scatter.9.cloned.1.call-start = ((), (), s32[]{:S(2)}) async-start(), calls=%async_computation.6 | async-start | bytes 4866048 | tf_op jit(solution)/shard_map/reduce_scatter | solution.py:397
  316.3 8.1 %copy-start.2 = (bf16[2048,768]{1,0:T(8,128)(2,1)S(1)}, bf16[2048,768]{1,0:T(8,128)(2,1)}, u32[]{:S(2)}) copy-start(bf16[2048,768]{1,0:T(8,128)(2,1)} %tokens_ref.1) | copy-start | bytes 9437188
  324.4 12.5 %copy-start.4 = (f32[4,1792]{1,0:T(4,128)S(1)}, f32[4,1792]{1,0:T(4,128)}, u32[]{:S(2)}) copy-start(f32[4,1792]{1,0:T(4,128)} %get-tuple-element.37) | copy-start | bytes 86020
  324.4 54.4 %copy-start = (bf16[2048,768]{1,0:T(8,128)(2,1)S(1)}, bf16[2048,768]{1,0:T(8,128)(2,1)}, u32[]{:S(2)}) copy-start(bf16[2048,768]{1,0:T(8,128)(2,1)} %param.25) | copy-start | bytes 9437188
  378.8 6.0 %copy-start.3 = (bf16[2048,768]{1,0:T(8,128)(2,1)S(1)}, bf16[2048,768]{1,0:T(8,128)(2,1)}, u32[]{:S(2)}) copy-start(bf16[2048,768]{1,0:T(8,128)(2,1)} %tokens_ref.1) | copy-start | bytes 9437188
  378.8 6.8 %copy-start.8 = (bf16[1536,768]{1,0:T(8,128)(2,1)S(1)}, bf16[1536,768]{1,0:T(8,128)(2,1)}, u32[]{:S(2)}) copy-start(bf16[1536,768]{1,0:T(8,128)(2,1)} %all-gather.5.cloned.1.call-done.wout_ref) | copy-start | bytes 7077892
Sparse Core Ops, SparseCore 0:
  12.0 68.2 all-gather.2
  83.2 56.1 all-gather.4
  222.7 106.0 reduce-scatter.6
  335.2 111.8 reduce-scatter.10
  453.9 106.1 reduce-scatter.8
